TPU v7x, 32 devices: a whole 2x2x4 slice. The times are simulated.
32 devices in a mesh: grp: 4 (over x, core), blk: 8 (over z, y).
Axes of the slice: x: 2, y: 2, z: 4, core: 2. Of those that a mesh axis runs over, the one named last changes fastest.
Arguments:
- stamps: float32 [32, 32, 64, 128], P(('grp', 'blk')), may hold values from -1 to 1
- stamp_target: int32 [32, 32, 128], P(('grp', 'blk')), may hold values from 0 to 4095
- pair_counts: int32 [32, 32], P(('grp', 'blk')), may hold values from 0 to 128, as said below
- conductance: float32 [8, 8192], P(None, ('grp', 'blk')), may hold values from 4 to 12
- block_cols: int32 [16, 8192], P(None, ('grp', 'blk')), may hold values from 0 to 8191, as said below
- newton_residual: float32 [8, 8192], P(None, ('grp', 'blk')), may hold values from -30 to 30
Outputs:
- update: float32 [8, 8192], P(None, ('grp', 'blk'))
- jacobian_blocks: float32 [16, 8, 8, 8192], P(None, None, None, ('grp', 'blk'))
- preconditioned_rhs: float32 [8, 8192], P(None, ('grp', 'blk'))
Inputs may be any that keep to these rules, and one draw needn't show every extreme that they name: `stamp_target`: A stamp's target is its block slot times 256 plus its block row local to the owner. `pair_counts`: every device sends exactly 128 live blocks to itself and exactly 128 to the next device in the order of grp+blk (the last device to the first), and at most 32 to every other owner; one owner drawn from the seed receives exactly 32 from every device other than itself and the device before it. `block_cols`: slot 0 of block row n names n itself; slots 1 to 7 name rows of the same group of 2048 rows as n; over the 256 block rows of one device, the slots from 8 on name rows owned by each device exactly 64 times.
All inputs are finite; a program needn't handle non-finite values.
Results may differ from a plain program's by a relative error of at most 0.0003.
Values sent between devices are 32-bit elements; how exact they have to be, the bound alone decides.
No kernel may reach another device: no remote copies, remote signals or barrier semaphores. Data moves between devices by JAX's collectives and lax.ppermute only.
A program may use at most 128 MiB of HBM per device.

v0:
```python
import functools

import jax
import jax.numpy as jnp
from jax import lax
from jax.experimental import pallas as pl
from jax.experimental.pallas import tpu as pltpu
from jax.sharding import PartitionSpec as P

K = 16
KRYLOV = 5
LOW = 32
EPS = 1e-06
LANES = 128
AXES = ("grp", "blk")

F32 = jnp.float32
BF16 = jnp.bfloat16
I32 = jnp.int32

LANE_GATHER = lax.GatherDimensionNumbers(
    offset_dims=(),
    collapsed_slice_dims=(1,),
    start_index_map=(1,),
    operand_batching_dims=(0,),
    start_indices_batching_dims=(0,),
)


def lane_gather(source, lanes):
    return lax.gather(
        source,
        lanes[..., None],
        LANE_GATHER,
        slice_sizes=(1, 1),
        mode=lax.GatherScatterMode.PROMISE_IN_BOUNDS,
    )


def my_place(members):
    first = lax.axis_index("grp") * members
    return first + lax.axis_index("blk"), first


def call(kernel, out_shape, *args, scratch=(), vmem=32 * 2**20):
    return pl.pallas_call(
        kernel,
        out_shape=out_shape,
        in_specs=[pl.BlockSpec(memory_space=pltpu.VMEM)] * len(args),
        out_specs=jax.tree.map(lambda _: pl.BlockSpec(memory_space=pltpu.VMEM), out_shape),
        scratch_shapes=list(scratch),
        compiler_params=pltpu.CompilerParams(vmem_limit_bytes=vmem),
    )(*args)


def iota(shape, axis):
    return lax.broadcasted_iota(I32, shape, axis)


def halves_of(rows):
    return rows // LANES


def half(index):
    return slice(index * LANES, (index + 1) * LANES)


def stack_rows(rows):
    sub = iota((8, LANES), 0)
    out = jnp.zeros((8, LANES), F32)
    for a, value in enumerate(rows):
        out = jnp.where(sub == a, jnp.sum(value, axis=0, keepdims=True), out)
    return out


def apply_inverse(inv_ref, vector):
    out = []
    for h, value in enumerate(vector):
        out.append(stack_rows([inv_ref[a, :, half(h)] * value for a in range(8)]))
    return out


def couple(jac_ref, picks, first, last, acc):
    count = len(acc)
    for k in range(first, last):
        for h in range(count):
            picked = jnp.zeros((8, LANES), F32)
            for index_ref, base, sources in picks:
                index = index_ref[k - base, :, half(h)]
                at, lanes = index >> 7, index & (LANES - 1)
                for s, source in enumerate(sources):
                    picked = jnp.where(at == s, lane_gather(source(), lanes), picked)
            for a in range(8):
                acc[h][a] = acc[h][a] + jac_ref[k, a, :, half(h)] * picked
    return acc


def zero_acc(count):
    return [[jnp.zeros((8, LANES), F32) for _ in range(8)] for _ in range(count)]


def block_sources(ref, first, members, count):
    return [(lambda d=d, h=h: ref[first + d, :, half(h)]) for d in range(members) for h in range(count)]


def store(ref, vector):
    for h, value in enumerate(vector):
        ref[:, half(h)] = value


def spread(ref, vector):
    for d in range(ref.shape[0]):
        for h, value in enumerate(vector):
            ref[d, :, half(h)] = value


def load(ref):
    return [ref[:, half(h)] for h in range(halves_of(ref.shape[1]))]


def dots_block(pairs):
    sub, lane = iota((8, LANES), 0), iota((8, LANES), 1)
    blocks = []
    for start in (0, 8):
        rows = jnp.zeros((8, LANES), F32)
        for i, (left, right) in enumerate(pairs[start : start + 8]):
            total = sum(x * y for x, y in zip(left, right))
            rows = jnp.where(sub == i, jnp.sum(total, axis=0, keepdims=True), rows)
        blocks.append(jnp.sum(rows, axis=1, keepdims=True))
    return jnp.where(lane < 96, blocks[0], blocks[1])


def read_dots(total, count):
    lane = iota((8, LANES), 1)
    out = []
    for at in (64, 96):
        column = jnp.sum(jnp.where(lane == at, total, 0.0), axis=1, keepdims=True)
        column = jnp.broadcast_to(column, (8, LANES))
        out += [jnp.broadcast_to(column[i : i + 1, :], (8, LANES)) for i in range(8)]
    return out[:count]


def pack_kernel(
    members,
    stamps_any,
    target_ref,
    counts_ref,
    cols_ref,
    send_ref,
    next_ref,
    own_ref,
    near_ref,
    pos_ref,
    stamps_ref,
    arrival,
):
    copy = pltpu.make_async_copy(stamps_any, stamps_ref, arrival)
    copy.start()
    devices = stamps_ref.shape[0]
    local_rows = cols_ref.shape[1]
    far_slots = K - K // 2
    per_owner = far_slots * local_rows // devices
    me, first = my_place(members)
    nxt = jnp.where(me + 1 == devices, 0, me + 1)
    group_start, group_rows = first * local_rows, members * local_rows
    lane = iota((1, LANES), 1)

    ids, slots = iota((devices, LANES), 0), iota((devices, LANES), 1)
    counts = jnp.broadcast_to(counts_ref[...], (devices, devices))
    diagonal = iota((devices, devices), 0) == iota((devices, devices), 1)
    counts = jnp.sum(jnp.where(diagonal, counts, 0).astype(F32), axis=1, keepdims=True)
    target = jnp.where(slots.astype(F32) < counts, target_ref[...].astype(F32), -1.0)
    low = jnp.where((ids == me) | (ids == nxt) | (slots >= LOW), -1.0, target)

    owners = iota((devices, LANES), 0)
    before = (iota((LANES, LANES), 0) < iota((LANES, LANES), 1)).astype(BF16)
    running = jnp.zeros((devices, 1), F32)
    asked = jnp.zeros((devices, LANES), F32)
    tiled = iota((LANES, LANES), 0) - 64
    for k in range(far_slots):
        for h in range(halves_of(local_rows)):
            cols = cols_ref[K // 2 + k : K // 2 + k + 1, half(h)]
            owner = cols // local_rows
            row = cols - owner * local_rows
            hot = (owners == owner).astype(F32)
            ahead = jnp.dot(hot.astype(BF16), before, preferred_element_type=F32) + running
            running = running + jnp.sum(hot, axis=1, keepdims=True)
            rank = jnp.sum(hot * ahead, axis=0, keepdims=True).astype(I32)
            asked += lax.dot_general(
                (hot * row.astype(F32)).astype(BF16),
                (tiled == rank).astype(F32).astype(BF16),
                (((1,), (1,)), ((), ())),
                preferred_element_type=F32,
            )
            near = (cols >= group_start) & (cols < group_start + group_rows)
            pos = jnp.where(near, -1, owner * per_owner + rank)
            pos_ref[k, :, half(h)] = jnp.broadcast_to(pos, (8, LANES))

    copy.wait()
    for ref, at in ((next_ref, nxt), (own_ref, me)):
        ref[0:64, :] = stamps_ref[at]
        row = jnp.sum(jnp.where(ids == at, target, 0.0), axis=0, keepdims=True)
        ref[64:72, :] = jnp.broadcast_to(row, (8, LANES))
    for d in range(devices):
        packed = jnp.zeros((16, LANES), F32)
        for g in range(4):
            piece = stamps_ref[d, 16 * g : 16 * g + 16, :]
            if g:
                piece = pltpu.roll(piece, LOW * g, 1)
            packed = jnp.where(lane // LOW == g, piece, packed)
        for i in range(8):
            send_ref[d, i] = packed[2 * i : 2 * i + 2, :]
        ints = jnp.where(lane < 64, low[d : d + 1, :], asked[d : d + 1, :])
        send_ref[d, 8] = jnp.broadcast_to(ints, (2, LANES))

    for k in range(K):
        for h in range(halves_of(local_rows)):
            cols = cols_ref[k : k + 1, half(h)]
            near = (cols >= group_start) & (cols < group_start + group_rows)
            near_ref[k, :, half(h)] = jnp.broadcast_to(jnp.where(near, cols - group_start, -1), (8, LANES))


def assemble_kernel(
    recv_ref, prev_ref, own_ref, cond_ref, resid_ref, whole_ref, jac_ref, inv_ref, served_ref, z_ref, left_ref, right_ref
):
    devices = recv_ref.shape[0]
    local_rows = cond_ref.shape[1]
    lane = iota((1, LANES), 1)
    blocks = devices // 4 + 2

    def stamp_rows(d):
        return jnp.concatenate([recv_ref[d, i] for i in range(8)], axis=0)

    def block(q):
        if q == 0:
            return own_ref[0:64, :], own_ref[64:65, :]
        if q == 1:
            return prev_ref[0:64, :], prev_ref[64:65, :]
        first = 4 * (q - 2)
        rows = []
        pieces = [stamp_rows(first + j) for j in range(4)]
        for g in range(4):
            out = jnp.zeros((16, LANES), F32)
            for j in range(4):
                piece = pieces[j]
                if j != g:
                    piece = pltpu.roll(piece, (LOW * (j - g)) % LANES, 1)
                out = jnp.where(lane // LOW == j, piece, out)
            rows.append(out)
        target = jnp.full((1, LANES), -1.0, F32)
        for j in range(4):
            piece = recv_ref[first + j, 8, 0:1, :]
            if j:
                piece = pltpu.roll(piece, LOW * j, 1)
            target = jnp.where(lane // LOW == j, piece, target)
        return jnp.concatenate(rows, axis=0), target

    most = 10
    for start in range(0, blocks, most):
        stop = min(start + most, blocks)
        width = 2 * (stop - start) * LANES
        values = []
        for q in range(start, stop):
            at = 2 * (q - start) * LANES
            stamp, target = block(q)
            target = target.astype(I32)
            slot, row = target >> (local_rows.bit_length() - 1), target & (local_rows - 1)
            hot = (iota((local_rows, LANES), 0) == row).astype(F32).astype(BF16)
            right_ref[:, at : at + LANES] = hot
            right_ref[:, at + LANES : at + 2 * LANES] = hot
            high = stamp.astype(BF16)
            low = (stamp - high.astype(F32)).astype(BF16)
            values.append((at, slot, high, low))

        for k in range(K):
            for at, slot, high, low in values:
                mask = (slot == k).astype(F32).astype(BF16)
                left_ref[64 * k : 64 * k + 64, at : at + LANES] = high * mask
                left_ref[64 * k : 64 * k + 64, at + LANES : at + 2 * LANES] = low * mask
        total = lax.dot_general(
            left_ref[:, 0:width],
            right_ref[:, 0:width],
            (((1,), (1,)), ((), ())),
            preferred_element_type=F32,
        ).reshape(K, 8, 8, local_rows)
        if start == 0:
            jac_ref[...] = total
        else:
            jac_ref[...] += total
    sub = iota((8, local_rows), 0)
    for a in range(8):
        jac_ref[0, a] = jac_ref[0, a] + jnp.where(sub == a, cond_ref[a : a + 1, :], 0.0)

    whole_ref[...] = jac_ref[...]

    work = [jac_ref[0, a] for a in range(8)]
    inverse = [jnp.where(sub == a, 1.0, 0.0).astype(F32) for a in range(8)]
    for p in range(8):
        scale = 1.0 / work[p][p : p + 1, :]
        top_work, top_inverse = work[p] * scale, inverse[p] * scale
        for a in range(8):
            if a != p:
                factor = work[a][p : p + 1, :]
                work[a] = work[a] - factor * top_work
                inverse[a] = inverse[a] - factor * top_inverse
        work[p], inverse[p] = top_work, top_inverse
    for a in range(8):
        inv_ref[a] = inverse[a]

    for d in range(devices):
        asked = pltpu.roll(recv_ref[d, 8, 0:1, :], 64, 1).astype(I32)
        served_ref[d] = jnp.broadcast_to(asked, (8, LANES))
    rhs = [-value for value in load(resid_ref)]
    spread(z_ref, apply_inverse(inv_ref, rhs) + [dots_block([(rhs, rhs)])])


def first_sweep_kernel(rhs, group_ref, vector_ref, jac_ref, inv_ref, near_ref, z_ref, dots_ref):
    vector = load(vector_ref)
    if rhs:
        vector = [-value for value in vector]
    members, count = group_ref.shape[0], len(vector)
    sources = block_sources(group_ref, 0, members, count)
    acc = couple(jac_ref, [(near_ref, 0, sources)], 1, K, zero_acc(count))
    spread(z_ref, apply_inverse(inv_ref, [v - stack_rows(c) for v, c in zip(vector, acc)]))
    dots_ref[0] = combine([group_ref[d, :, half(count)] for d in range(members)])
    dots_ref[1] = group_ref[lax.axis_index("blk"), :, half(count)]


def second_sweep_kernel(
    rhs,
    group_ref,
    vector_ref,
    jac_ref,
    inv_ref,
    near_ref,
    served_ref,
    dots_ref,
    send_ref,
    coupled_ref,
):
    vector = load(vector_ref)
    if rhs:
        vector = [-value for value in vector]
    members, count = group_ref.shape[0], len(vector)
    sources = block_sources(group_ref, 0, members, count)
    acc = couple(jac_ref, [(near_ref, 0, sources)], 1, K, zero_acc(count))
    coupled = [stack_rows(c) for c in acc]
    result = apply_inverse(inv_ref, [v - c for v, c in zip(vector, coupled)])
    store(coupled_ref, coupled)
    dots = dots_ref[1]
    lane = iota((8, LANES), 1)
    for d in range(send_ref.shape[0]):
        index = served_ref[d]
        lanes = index & (LANES - 1)
        picked = lane_gather(result[0], lanes)
        for h in range(1, count):
            picked = jnp.where(index >> 7 == h, lane_gather(result[h], lanes), picked)
        send_ref[d, :, half(0)] = jnp.where(lane < 64, picked, dots)
        for h in range(1, count):
            send_ref[d, :, half(h)] = result[h]
    _, first = my_place(members)
    for d in range(members):
        send_ref[first + d, :, half(0)] = result[0]


def combine(terms):
    return functools.reduce(lambda x, y: x + y, terms)


def orthogonalize(dots, step, gram):
    count = step + 1
    for i in range(count):
        gram[(i, step)] = gram[(step, i)] = dots[i]
    along = dots[count : 2 * count]
    hess = [gram[(i, step)] + along[i] for i in range(count)]
    coefs = [(1.0 - h if i == step else -h) for i, h in enumerate(hess)]
    square = dots[2 * count]
    for i in range(count):
        inner = combine([coefs[l] * gram[(i, l)] for l in range(count)])
        square = square + coefs[i] * (2.0 * along[i] + inner)
    length = jnp.sqrt(jnp.maximum(square, 0.0) + EPS)
    return hess, length, coefs


def read_scalars(refs):
    gram, hess, lengths = {}, {}, []
    beta = refs[0][0]
    for step, ref in enumerate(refs[1:]):
        count = step + 1
        for i in range(count):
            gram[(i, step)] = gram[(step, i)] = ref[i]
            hess[(i, step)] = ref[count + i]
        hess[(count, step)] = ref[2 * count]
    return beta, gram, hess


def operate_kernel(step, members, recv_ref, group_dots_ref, coupled_ref, vector_ref, *refs):
    jac_ref, inv_ref, near_ref, pos_ref = refs[:4]
    refs = refs[4:]
    states, scalar_refs = refs[:step], refs[step : 2 * step]
    state_ref, scalars_ref, vector_out_ref, z_ref = refs[2 * step :]
    devices = recv_ref.shape[0]
    rows = coupled_ref.shape[1]
    count = halves_of(rows)
    per_owner = (K - K // 2) * rows // devices
    each = LANES // per_owner
    lane = iota((8, LANES), 1)
    me, first = my_place(members)

    arrived = []
    total = group_dots_ref[0]
    for q in range(devices // each):
        out = recv_ref[q * each, :, half(0)]
        for j in range(each):
            d = q * each + j
            piece = recv_ref[d, :, half(0)]
            outside = (d < first) | (d >= first + members)
            total = total + jnp.where(outside, piece, 0.0)
            if j:
                out = jnp.where(lane // per_owner == j, pltpu.roll(piece, j * per_owner, 1), out)
        arrived.append(out)

    near = (near_ref, 0, block_sources(recv_ref, first, members, count))
    acc = couple(jac_ref, [near], 1, K // 2, zero_acc(count))
    acc = couple(jac_ref, [near, (pos_ref, K // 2, [(lambda v=v: v) for v in arrived])], K // 2, K, acc)
    image = [stack_rows(c) - n for c, n in zip(acc, load(coupled_ref))]
    search = [recv_ref[me, :, half(h)] for h in range(count)]
    vector = load(vector_ref)

    if step == 0:
        vector = [-value for value in vector]
        length = jnp.sqrt(read_dots(total, 1)[0] + EPS)
        scalars_ref[0] = length
        coefs = []
    else:
        _, gram, _ = read_scalars(scalar_refs)
        dots = read_dots(total, 2 * step + 1)
        hess, length, coefs = orthogonalize(dots, step - 1, gram)
        for i in range(step):
            scalars_ref[i] = gram[(i, step - 1)]
            scalars_ref[step + i] = hess[i]
        scalars_ref[2 * step] = length
    scale = 1.0 / length

    def recombine(part, fresh):
        out = []
        for h, value in enumerate(fresh):
            for c, ref in zip(coefs, states):
                value = value + c * ref[part, :, half(h)]
            value = value * scale
            state_ref[part, :, half(h)] = value
            out.append(value)
        return out

    basis = [[ref[0, :, half(h)] for h in range(count)] for ref in states]
    basis.append(recombine(0, vector))
    recombine(1, search)
    image = recombine(2, image)
    store(vector_out_ref, image)
    pairs = [(b, basis[-1]) for b in basis] + [(b, image) for b in basis] + [(image, image)]
    block = dots_block(pairs)
    spread(z_ref, apply_inverse(inv_ref, image) + [block] if step + 1 < KRYLOV else [block])


def finish_kernel(dots_ref, *refs):
    states, scalar_refs = refs[:KRYLOV], refs[KRYLOV : 2 * KRYLOV]
    update_ref, first_ref = refs[2 * KRYLOV :]
    total = combine([dots_ref[d] for d in range(dots_ref.shape[0])])
    beta, gram, hess = read_scalars(scalar_refs)
    last, length, _ = orthogonalize(read_dots(total, 2 * KRYLOV + 1), KRYLOV - 1, gram)
    for i, value in enumerate(last):
        hess[(i, KRYLOV - 1)] = value
    hess[(KRYLOV, KRYLOV - 1)] = length

    work = [
        [combine([hess[(l, i)] * hess[(l, j)] for l in range(min(i, j) + 2)]) for j in range(KRYLOV)]
        for i in range(KRYLOV)
    ]
    vector = [beta * hess[(0, j)] for j in range(KRYLOV)]
    for p in range(KRYLOV):
        scale = 1.0 / work[p][p]
        top_work = [value * scale for value in work[p]]
        top = vector[p] * scale
        for i in range(KRYLOV):
            if i != p:
                factor = work[i][p]
                work[i] = [w - factor * t for w, t in zip(work[i], top_work)]
                vector[i] = vector[i] - factor * top
        work[p], vector[p] = top_work, top
    for h in range(halves_of(update_ref.shape[1])):
        update_ref[:, half(h)] = combine([c * ref[1, :, half(h)] for c, ref in zip(vector, states)])
        first_ref[:, half(h)] = beta * states[0][1, :, half(h)]


def shape(*dims, dtype=F32):
    return jax.ShapeDtypeStruct(dims, dtype)


def exchange(array, axes):
    return lax.all_to_all(array, axes, split_axis=0, concat_axis=0, tiled=True)


def local(stamps, stamp_target, pair_counts, conductance, block_cols, newton_residual):
    members = lax.axis_size("blk")
    devices = lax.axis_size("grp") * members
    rows = conductance.shape[1]

    send, to_next, own, near, pos = pl.pallas_call(
        functools.partial(pack_kernel, members),
        out_shape=(
            shape(devices, 9, 2, LANES),
            shape(72, LANES),
            shape(72, LANES),
            shape(K, 8, rows, dtype=I32),
            shape(K - K // 2, 8, rows, dtype=I32),
        ),
        in_specs=[pl.BlockSpec(memory_space=space) for space in (pl.ANY,) + 3 * (pltpu.VMEM,)],
        out_specs=tuple(pl.BlockSpec(memory_space=pltpu.VMEM) for _ in range(5)),
        scratch_shapes=[pltpu.VMEM(stamps.shape[1:], F32), pltpu.SemaphoreType.DMA],
        compiler_params=pltpu.CompilerParams(vmem_limit_bytes=60 * 2**20),
    )(stamps[0], stamp_target[0], pair_counts, block_cols)
    got = exchange(send, AXES)
    prev = lax.ppermute(to_next, AXES, [(i, (i + 1) % devices) for i in range(devices)])

    width = 2 * LANES * min(devices // 4 + 2, 10)
    jacobian, blocks, inverse, served, z = call(
        assemble_kernel,
        (
            shape(K, 8, 8, rows),
            shape(K, 8, 8, rows),
            shape(8, 8, rows),
            shape(devices, 8, LANES, dtype=I32),
            shape(members, 8, rows + LANES),
        ),
        got,
        prev,
        own,
        conductance,
        newton_residual,
        scratch=(pltpu.VMEM((64 * K, width), BF16), pltpu.VMEM((rows, width), BF16)),
    )

    states, scalars = [], []
    vector = newton_residual
    for step in range(KRYLOV):
        rhs = step == 0
        z, group_dots = call(
            functools.partial(first_sweep_kernel, rhs),
            (shape(members, 8, rows), shape(2, 8, LANES)),
            exchange(z, "blk"),
            vector,
            blocks,
            inverse,
            near,
        )
        send, coupled = call(
            functools.partial(second_sweep_kernel, rhs),
            (shape(devices, 8, rows), shape(8, rows)),
            exchange(z, "blk"),
            vector,
            blocks,
            inverse,
            near,
            served,
            group_dots,
        )
        last = step + 1 == KRYLOV
        state, scalar, vector, z = call(
            functools.partial(operate_kernel, step, members),
            (
                shape(3, 8, rows),
                shape(2 * step + 1, 8, LANES),
                shape(8, rows),
                shape(devices, 8, LANES) if last else shape(members, 8, rows + LANES),
            ),
            exchange(send, AXES),
            group_dots,
            coupled,
            vector,
            blocks,
            inverse,
            near,
            pos,
            *states,
            *scalars,
        )
        states.append(state)
        scalars.append(scalar)

    update, first = call(finish_kernel, (shape(8, rows), shape(8, rows)), exchange(z, AXES), *states, *scalars)
    return update, jacobian, first


def solution(mesh):
    placed = (
        P(AXES, None, None, None),
        P(AXES, None, None),
        P(AXES, None),
        P(None, AXES),
        P(None, AXES),
        P(None, AXES),
    )
    return jax.shard_map(
        local,
        mesh=mesh,
        in_specs=placed,
        out_specs=(P(None, AXES), P(None, None, None, AXES), P(None, AXES)),
        check_vma=False,
    )
```

profile of v0, /device:TPU:0, one launch (start us, length us, event | category | flops | bytes accessed | tf_op | source)
XLA Modules:
  0.0 208.9 jit_solution(953100354528626113)
XLA Ops:
  0.6 3.0 %shard_map.85 = (f32[32,9,2,128]{3,2,1,0:T(2,128)}, f32[72,128]{1,0:T(8,128)}, f32[72,128]{1,0:T(8,128)}, s32[16,8,256]{2,1,0:T(8,128)}, s32[8,8,256]{2,1,0:T(8,128)}) custom-call(f32[32,64,128]{2,1,0:T(8,128)} %bitcast.2, s32[32,128]{1,0:T(8,128)} %bitcast.3, s32[1,32]{1,0:T(1,128)} %counts_ref.1, s32[16,256]{1,0:T(8,128)} %cols_ref.1), custom_call_target="tpu_custom_call" | custom-call | tf_op jit(solution)/shard_map/pallas_call | solution.py:508
  3.7 7.3 %all-to-all-start = ((f32[32,9,2,128]{3,2,1,0:T(2,128)}), f32[32,9,2,128]{3,2,1,0:T(2,128)S(1)}, u32[]{:S(2)}, u32[]{:S(2)}) async-start(f32[32,9,2,128]{3,2,1,0:T(2,128)} %get-tuple-element.54), calls=%async_computation | async-start | bytes 589824 | tf_op jit(solution)/shard_map/all_to_all | solution.py:500
  11.0 1.8 collective-permute-start
  12.9 9.8 %collective-permute-done.prev_ref = f32[72,128]{1,0:T(8,128)S(1)} collective-permute-done((f32[72,128]{1,0:T(8,128)S(1)}, f32[72,128]{1,0:T(8,128)S(1)}, u32[]{:S(2)}, u32[]{:S(2)}) %collective-permute-start) | collective-permute-done | bytes 36896 | tf_op jit(solution)/shard_map/ppermute | solution.py:523
  23.3 2.7 %shard_map.86 = (f32[16,8,8,256]{3,2,1,0:T(8,128)}, f32[16,8,8,256]{3,2,1,0:T(8,128)S(1)}, f32[8,8,256]{2,1,0:T(8,128)S(1)}, s32[32,8,128]{2,1,0:T(8,128)S(1)}, f32[8,8,384]{2,1,0:T(8,128)S(1)}) custom-call(f32[32,9,2,128]{3,2,1,0:T(2,128)S(1)} %all-to-all-done.recv_ref, f32[72,128]{1,0:T(8,128)S(1)} %collective-permute-done.prev_ref, ...), custom_call_target="tpu_custom_call" | custom-call | tf_op jit(solution)/shard_map/pallas_call | solution.py:46
  26.0 9.6 %all_to_all.85.group_ref = f32[8,8,384]{2,1,0:T(8,128)S(1)} all-to-all(f32[8,8,384]{2,1,0:T(8,128)S(1)} %get-tuple-element.57), channel_id=1, replica_groups=mesh['grp'=4,'blk'=8] {'blk'}, dimensions={0} | all-to-all | bytes 196608 | tf_op jit(solution)/shard_map/all_to_all | solution.py:500
  36.4 9.3 %all_to_all.86.group_ref = f32[8,8,256]{2,1,0:T(8,128)S(1)} all-to-all(f32[8,8,256]{2,1,0:T(8,128)S(1)} %get-tuple-element.61), channel_id=1, replica_groups=mesh['grp'=4,'blk'=8] {'blk'}, dimensions={0} | all-to-all | bytes 131072 | tf_op jit(solution)/shard_map/all_to_all | solution.py:500
  45.7 0.9 shard_map.88
  46.6 12.5 %all_to_all.87.recv_ref = f32[32,8,256]{2,1,0:T(8,128)S(1)} all-to-all(f32[32,8,256]{2,1,0:T(8,128)S(1)} %get-tuple-element.64), channel_id=1, replica_groups=mesh['grp'=4,'blk'=8] {'grp','blk'}, dimensions={0} | all-to-all | bytes 524288 | tf_op jit(solution)/shard_map/all_to_all | solution.py:500
  59.1 1.2 shard_map.89
  60.2 10.0 %all_to_all.88.group_ref = f32[8,8,384]{2,1,0:T(8,128)S(1)} all-to-all(f32[8,8,384]{2,1,0:T(8,128)S(1)} %get-tuple-element.67), channel_id=1, replica_groups=mesh['grp'=4,'blk'=8] {'blk'}, dimensions={0} | all-to-all | bytes 196608 | tf_op jit(solution)/shard_map/all_to_all | solution.py:500
  70.9 9.3 %all_to_all.89.group_ref = f32[8,8,256]{2,1,0:T(8,128)S(1)} all-to-all(f32[8,8,256]{2,1,0:T(8,128)S(1)} %get-tuple-element.69), channel_id=1, replica_groups=mesh['grp'=4,'blk'=8] {'blk'}, dimensions={0} | all-to-all | bytes 131072 | tf_op jit(solution)/shard_map/all_to_all | solution.py:500
  80.2 0.9 shard_map.91
  81.1 12.4 %all_to_all.90.recv_ref = f32[32,8,256]{2,1,0:T(8,128)S(1)} all-to-all(f32[32,8,256]{2,1,0:T(8,128)S(1)} %get-tuple-element.71), channel_id=1, replica_groups=mesh['grp'=4,'blk'=8] {'grp','blk'}, dimensions={0} | all-to-all | bytes 524288 | tf_op jit(solution)/shard_map/all_to_all | solution.py:500
  93.5 1.1 shard_map.92
  94.6 10.0 %all_to_all.91.group_ref = f32[8,8,384]{2,1,0:T(8,128)S(1)} all-to-all(f32[8,8,384]{2,1,0:T(8,128)S(1)} %get-tuple-element.75), channel_id=1, replica_groups=mesh['grp'=4,'blk'=8] {'blk'}, dimensions={0} | all-to-all | bytes 196608 | tf_op jit(solution)/shard_map/all_to_all | solution.py:500
  105.3 9.3 %all_to_all.92.group_ref = f32[8,8,256]{2,1,0:T(8,128)S(1)} all-to-all(f32[8,8,256]{2,1,0:T(8,128)S(1)} %get-tuple-element.77), channel_id=1, replica_groups=mesh['grp'=4,'blk'=8] {'blk'}, dimensions={0} | all-to-all | bytes 131072 | tf_op jit(solution)/shard_map/all_to_all | solution.py:500
  114.6 0.9 shard_map.94
  115.5 12.4 %all_to_all.93.recv_ref = f32[32,8,256]{2,1,0:T(8,128)S(1)} all-to-all(f32[32,8,256]{2,1,0:T(8,128)S(1)} %get-tuple-element.79), channel_id=1, replica_groups=mesh['grp'=4,'blk'=8] {'grp','blk'}, dimensions={0} | all-to-all | bytes 524288 | tf_op jit(solution)/shard_map/all_to_all | solution.py:500
  127.9 1.2 shard_map.95
  129.0 10.0 %all_to_all.94.group_ref = f32[8,8,384]{2,1,0:T(8,128)S(1)} all-to-all(f32[8,8,384]{2,1,0:T(8,128)S(1)} %get-tuple-element.83), channel_id=1, replica_groups=mesh['grp'=4,'blk'=8] {'blk'}, dimensions={0} | all-to-all | bytes 196608 | tf_op jit(solution)/shard_map/all_to_all | solution.py:500
  139.7 9.3 %all_to_all.95.group_ref = f32[8,8,256]{2,1,0:T(8,128)S(1)} all-to-all(f32[8,8,256]{2,1,0:T(8,128)S(1)} %get-tuple-element.85), channel_id=1, replica_groups=mesh['grp'=4,'blk'=8] {'blk'}, dimensions={0} | all-to-all | bytes 131072 | tf_op jit(solution)/shard_map/all_to_all | solution.py:500
  149.0 0.9 shard_map.97
  149.9 12.4 %all_to_all.96.recv_ref = f32[32,8,256]{2,1,0:T(8,128)S(1)} all-to-all(f32[32,8,256]{2,1,0:T(8,128)S(1)} %get-tuple-element.87), channel_id=1, replica_groups=mesh['grp'=4,'blk'=8] {'grp','blk'}, dimensions={0} | all-to-all | bytes 524288 | tf_op jit(solution)/shard_map/all_to_all | solution.py:500
  162.3 1.2 shard_map.98
  163.4 10.0 %all_to_all.97.group_ref = f32[8,8,384]{2,1,0:T(8,128)S(1)} all-to-all(f32[8,8,384]{2,1,0:T(8,128)S(1)} %get-tuple-element.91), channel_id=1, replica_groups=mesh['grp'=4,'blk'=8] {'blk'}, dimensions={0} | all-to-all | bytes 196608 | tf_op jit(solution)/shard_map/all_to_all | solution.py:500
  174.2 9.3 %all_to_all.98.group_ref = f32[8,8,256]{2,1,0:T(8,128)S(1)} all-to-all(f32[8,8,256]{2,1,0:T(8,128)S(1)} %get-tuple-element.93), channel_id=1, replica_groups=mesh['grp'=4,'blk'=8] {'blk'}, dimensions={0} | all-to-all | bytes 131072 | tf_op jit(solution)/shard_map/all_to_all | solution.py:500
  183.4 0.9 shard_map.100
  184.4 12.4 %all_to_all.99.recv_ref = f32[32,8,256]{2,1,0:T(8,128)S(1)} all-to-all(f32[32,8,256]{2,1,0:T(8,128)S(1)} %get-tuple-element.95), channel_id=1, replica_groups=mesh['grp'=4,'blk'=8] {'grp','blk'}, dimensions={0} | all-to-all | bytes 524288 | tf_op jit(solution)/shard_map/all_to_all | solution.py:500
  196.7 1.7 shard_map.101
  198.4 9.8 %all_to_all.100.dots_ref = f32[32,8,128]{2,1,0:T(8,128)S(1)} all-to-all(f32[32,8,128]{2,1,0:T(8,128)S(1)} %get-tuple-element.99), channel_id=1, replica_groups=mesh['grp'=4,'blk'=8] {'grp','blk'}, dimensions={0} | all-to-all | bytes 262144 | tf_op jit(solution)/shard_map/all_to_all | solution.py:500
  208.2 0.8 shard_map.102
  (18 shorter events, 4.3 us)
Async XLA Ops:
  3.7 7.4 %copy-start.5 = (f32[72,128]{1,0:T(8,128)S(1)}, f32[72,128]{1,0:T(8,128)}, u32[]{:S(2)}) copy-start(f32[72,128]{1,0:T(8,128)} %get-tuple-element.55) | copy-start | bytes 110596
  3.7 19.6 %copy-start.2 = (f32[8,256]{1,0:T(8,128)S(1)}, f32[8,256]{1,0:T(8,128)}, u32[]{:S(2)}) copy-start(f32[8,256]{1,0:T(8,128)} %vector_ref.5) | copy-start | bytes 24580
  3.7 19.6 %copy-start.3 = (f32[72,128]{1,0:T(8,128)S(1)}, f32[72,128]{1,0:T(8,128)}, u32[]{:S(2)}) copy-start(f32[72,128]{1,0:T(8,128)} %get-tuple-element.56.own_ref) | copy-start | bytes 110596
  3.7 19.6 %copy-start.4 = (f32[8,256]{1,0:T(8,128)S(1)}, f32[8,256]{1,0:T(8,128)}, u32[]{:S(2)}) copy-start(f32[8,256]{1,0:T(8,128)} %cond_ref.1) | copy-start | bytes 24580
  3.7 19.5 %all-to-all-start = ((f32[32,9,2,128]{3,2,1,0:T(2,128)}), f32[32,9,2,128]{3,2,1,0:T(2,128)S(1)}, u32[]{:S(2)}, u32[]{:S(2)}) async-start(f32[32,9,2,128]{3,2,1,0:T(2,128)} %get-tuple-element.54), calls=%async_computation | async-start | bytes 589824 | tf_op jit(solution)/shard_map/all_to_all | solution.py:500
  11.0 11.6 %collective-permute-start = (f32[72,128]{1,0:T(8,128)S(1)}, f32[72,128]{1,0:T(8,128)S(1)}, u32[]{:S(2)}, u32[]{:S(2)}) collective-permute-start(f32[72,128]{1,0:T(8,128)S(1)} %copy-done.5), channel_id=1, source_target_pairs={{0,1},{1,2},{2,3},{3,4},{4,5},{5,6},{6,7},{7,8},{8,9},{9,10},{10,1... | collective-permute-start | bytes 110600 | tf_op jit(solution)/shard_map/ppermute | solution.py:523
  26.0 9.6 %copy-start = (s32[16,8,256]{2,1,0:T(8,128)S(1)}, s32[16,8,256]{2,1,0:T(8,128)}, u32[]{:S(2)}) copy-start(s32[16,8,256]{2,1,0:T(8,128)} %get-tuple-element.60.near_ref.refs_2_) | copy-start | bytes 393220
  46.6 12.5 %copy-start.1 = (s32[8,8,256]{2,1,0:T(8,128)S(1)}, s32[8,8,256]{2,1,0:T(8,128)}, u32[]{:S(2)}) copy-start(s32[8,8,256]{2,1,0:T(8,128)} %get-tuple-element.66.refs_3_) | copy-start | bytes 196612
where the time goes:
time: 210 us; the launch traced here: 209 us
  blocking collectives  168 us (80%)
  Pallas kernels  21 us (10%)
  waiting for transfers between devices  10.4 us (5%)
  starting transfers between devices  9.13 us (4%)
    all_to_all x16, blocking collectives, exchange(): return lax.all_to_all(array, axes, split_axis=0, concat_axis=0, tiled=True)  168 us
    pallas_call x17, Pallas kernels, call(): pl.pallas_call(kernel, out_shape=out_shape, in_specs=[pl.BlockSpec(memory...  17.9 us
    ppermute x1, waiting for transfers between devices, local(): lax.ppermute(to_next, AXES, [(i, (i + 1) % devices) for i in range(device...  9.78 us
    all_to_all x1, starting transfers between devices, exchange(): return lax.all_to_all(array, axes, split_axis=0, concat_axis=0, tiled=True)  7.3 us
  transfers between devices with their start and end apart: 2, of which 2 were waited for; matrix products, arithmetic and copies ran while one was open for 0% of the time, Pallas kernels for 0%

commit v1 on v0

--- a/solution.py
+++ b/solution.py
@@ -140,6 +140,26 @@
     return out[:count]
 
 
+def live_targets(target_ref, counts_ref):
+    devices = target_ref.shape[0]
+    counts = jnp.broadcast_to(counts_ref[...], (devices, devices))
+    diagonal = iota((devices, devices), 0) == iota((devices, devices), 1)
+    counts = jnp.sum(jnp.where(diagonal, counts, 0).astype(F32), axis=1, keepdims=True)
+    return jnp.where(iota((devices, LANES), 1).astype(F32) < counts, target_ref[...].astype(F32), -1.0)
+
+
+def next_kernel(members, stamps_any, target_ref, counts_ref, next_ref, arrival):
+    devices = stamps_any.shape[0]
+    me, _ = my_place(members)
+    nxt = jnp.where(me + 1 == devices, 0, me + 1)
+    copy = pltpu.make_async_copy(stamps_any.at[nxt], next_ref.at[0:64], arrival)
+    copy.start()
+    target = live_targets(target_ref, counts_ref)
+    row = jnp.sum(jnp.where(iota((devices, LANES), 0) == nxt, target, 0.0), axis=0, keepdims=True)
+    next_ref[64:72, :] = jnp.broadcast_to(row, (8, LANES))
+    copy.wait()
+
+
 def pack_kernel(
     members,
     stamps_any,
@@ -147,7 +167,6 @@
     counts_ref,
     cols_ref,
     send_ref,
-    next_ref,
     own_ref,
     near_ref,
     pos_ref,
@@ -166,10 +185,7 @@
     lane = iota((1, LANES), 1)
 
     ids, slots = iota((devices, LANES), 0), iota((devices, LANES), 1)
-    counts = jnp.broadcast_to(counts_ref[...], (devices, devices))
-    diagonal = iota((devices, devices), 0) == iota((devices, devices), 1)
-    counts = jnp.sum(jnp.where(diagonal, counts, 0).astype(F32), axis=1, keepdims=True)
-    target = jnp.where(slots.astype(F32) < counts, target_ref[...].astype(F32), -1.0)
+    target = live_targets(target_ref, counts_ref)
     low = jnp.where((ids == me) | (ids == nxt) | (slots >= LOW), -1.0, target)
 
     owners = iota((devices, LANES), 0)
@@ -197,10 +213,9 @@
             pos_ref[k, :, half(h)] = jnp.broadcast_to(pos, (8, LANES))
 
     copy.wait()
-    for ref, at in ((next_ref, nxt), (own_ref, me)):
-        ref[0:64, :] = stamps_ref[at]
-        row = jnp.sum(jnp.where(ids == at, target, 0.0), axis=0, keepdims=True)
-        ref[64:72, :] = jnp.broadcast_to(row, (8, LANES))
+    own_ref[0:64, :] = stamps_ref[me]
+    row = jnp.sum(jnp.where(ids == me, target, 0.0), axis=0, keepdims=True)
+    own_ref[64:72, :] = jnp.broadcast_to(row, (8, LANES))
     for d in range(devices):
         packed = jnp.zeros((16, LANES), F32)
         for g in range(4):
@@ -505,22 +520,30 @@
     devices = lax.axis_size("grp") * members
     rows = conductance.shape[1]
 
-    send, to_next, own, near, pos = pl.pallas_call(
+    to_next = pl.pallas_call(
+        functools.partial(next_kernel, members),
+        out_shape=shape(72, LANES),
+        in_specs=[pl.BlockSpec(memory_space=space) for space in (pl.ANY,) + 2 * (pltpu.VMEM,)],
+        out_specs=pl.BlockSpec(memory_space=pltpu.VMEM),
+        scratch_shapes=[pltpu.SemaphoreType.DMA],
+        compiler_params=pltpu.CompilerParams(vmem_limit_bytes=60 * 2**20),
+    )(stamps[0], stamp_target[0], pair_counts)
+    prev = lax.ppermute(to_next, AXES, [(i, (i + 1) % devices) for i in range(devices)])
+    send, own, near, pos = pl.pallas_call(
         functools.partial(pack_kernel, members),
         out_shape=(
             shape(devices, 9, 2, LANES),
-            shape(72, LANES),
             shape(72, LANES),
             shape(K, 8, rows, dtype=I32),
             shape(K - K // 2, 8, rows, dtype=I32),
         ),
         in_specs=[pl.BlockSpec(memory_space=space) for space in (pl.ANY,) + 3 * (pltpu.VMEM,)],
-        out_specs=tuple(pl.BlockSpec(memory_space=pltpu.VMEM) for _ in range(5)),
+        out_specs=tuple(pl.BlockSpec(memory_space=pltpu.VMEM) for _ in range(4)),
         scratch_shapes=[pltpu.VMEM(stamps.shape[1:], F32), pltpu.SemaphoreType.DMA],
         compiler_params=pltpu.CompilerParams(vmem_limit_bytes=60 * 2**20),
     )(stamps[0], stamp_target[0], pair_counts, block_cols)
+    send, prev = lax.optimization_barrier((send, prev))
     got = exchange(send, AXES)
-    prev = lax.ppermute(to_next, AXES, [(i, (i + 1) % devices) for i in range(devices)])
 
     width = 2 * LANES * min(devices // 4 + 2, 10)
     jacobian, blocks, inverse, served, z = call(

time: 210 us -> 213 us (1.014)
  blocking collectives: 168 us -> 182 us
  waiting for transfers between devices: 10.4 us -> 2.56 us
  starting transfers between devices: 9.13 us -> 3.02 us
    all_to_all x16 -> x17, blocking collectives: 168 us -> 182 us  [exchange(): return lax.all_to_all(array, axes, split_axis=0, concat_axis=0, tiled=True)]
    all_to_all x1 -> x0, starting transfers between devices: 7.3 us -> none  [exchange(): return lax.all_to_all(array, axes, split_axis=0, concat_axis=0, tiled=True)]
    ppermute x1, waiting for transfers between devices: 9.78 us -> 2.56 us  [local(): lax.ppermute(to_next, AXES, [(i, (i + 1) % devices) for i in range(device...]
  transfers between devices with their start and end apart: 2 -> 1, of which waited for: 2 -> 1; matrix products, arithmetic and copies ran while one was open for 0% -> 0% of each run, Pallas kernels for 0% -> 1%
where the time goes in v1:
time: 213 us; the launch traced here: 212 us
  blocking collectives  182 us (85%)
  Pallas kernels  23.1 us (11%)
  starting transfers between devices  3.02 us (1%)
  waiting for transfers between devices  2.56 us (1%)
    all_to_all x17, blocking collectives, exchange(): return lax.all_to_all(array, axes, split_axis=0, concat_axis=0, tiled=True)  182 us
    pallas_call x17, Pallas kernels, call(): pl.pallas_call(kernel, out_shape=out_shape, in_specs=[pl.BlockSpec(memory...  17.9 us
  transfers between devices with their start and end apart: 1, of which 1 were waited for; matrix products, arithmetic and copies ran while one was open for 0% of the time, Pallas kernels for 1%

profile of v1, /device:TPU:0, one launch (start us, length us, event | category | flops | bytes accessed | tf_op | source)
XLA Modules:
  0.0 211.9 jit_solution(2959428320092043749)
XLA Ops:
  0.6 2.1 shard_map.86
  2.7 3.0 %collective-permute-start = (f32[72,128]{1,0:T(8,128)}, f32[72,128]{1,0:T(8,128)S(1)}, u32[]{:S(2)}, u32[]{:S(2)}) collective-permute-start(f32[72,128]{1,0:T(8,128)} %shard_map.86), channel_id=1, source_target_pairs={{0,1},{1,2},{2,3},{3,4},{4,5},{5,6},{6,7},{7,8},{8,9},{9,10},{10,1... | collective-permute-start | bytes 110600 | tf_op jit(solution)/shard_map/ppermute | solution.py:531
  5.8 3.0 %shard_map.85 = (f32[32,9,2,128]{3,2,1,0:T(2,128)}, f32[72,128]{1,0:T(8,128)}, s32[16,8,256]{2,1,0:T(8,128)}, s32[8,8,256]{2,1,0:T(8,128)}) custom-call(f32[32,64,128]{2,1,0:T(8,128)} %bitcast.3, s32[32,128]{1,0:T(8,128)} %bitcast.5, s32[1,32]{1,0:T(1,128)} %counts_ref.3, s32[16,256]{1,0:T(8,128)} %cols_ref.1), custom_call_target="tpu_custom_call" | custom-call | tf_op jit(solution)/shard_map/pallas_call | solution.py:532
  8.8 2.6 %collective-permute-done.prev_ref = f32[72,128]{1,0:T(8,128)S(1)} collective-permute-done((f32[72,128]{1,0:T(8,128)}, f32[72,128]{1,0:T(8,128)S(1)}, u32[]{:S(2)}, u32[]{:S(2)}) %collective-permute-start) | collective-permute-done | bytes 36896 | tf_op jit(solution)/shard_map/ppermute | solution.py:531
  11.4 14.4 %all_to_all.85.recv_ref = f32[32,9,2,128]{3,2,1,0:T(2,128)S(1)} all-to-all(f32[32,9,2,128]{3,2,1,0:T(2,128)} %get-tuple-element.56), channel_id=1, replica_groups=mesh['grp'=4,'blk'=8] {'grp','blk'}, dimensions={0} | all-to-all | bytes 589824 | tf_op jit(solution)/shard_map/all_to_all | solution.py:515
  25.7 2.7 %shard_map.87 = (f32[16,8,8,256]{3,2,1,0:T(8,128)}, f32[16,8,8,256]{3,2,1,0:T(8,128)S(1)}, f32[8,8,256]{2,1,0:T(8,128)S(1)}, s32[32,8,128]{2,1,0:T(8,128)S(1)}, f32[8,8,384]{2,1,0:T(8,128)S(1)}) custom-call(f32[32,9,2,128]{3,2,1,0:T(2,128)S(1)} %all_to_all.85.recv_ref, f32[72,128]{1,0:T(8,128)S(1)} %collective-permute-done.prev_ref, ...), custom_call_target="tpu_custom_call" | custom-call | tf_op jit(solution)/shard_map/pallas_call | solution.py:46
  28.5 10.1 %all_to_all.86.group_ref = f32[8,8,384]{2,1,0:T(8,128)S(1)} all-to-all(f32[8,8,384]{2,1,0:T(8,128)S(1)} %get-tuple-element.59), channel_id=1, replica_groups=mesh['grp'=4,'blk'=8] {'blk'}, dimensions={0} | all-to-all | bytes 196608 | tf_op jit(solution)/shard_map/all_to_all | solution.py:515
  39.3 9.3 %all_to_all.87.group_ref = f32[8,8,256]{2,1,0:T(8,128)S(1)} all-to-all(f32[8,8,256]{2,1,0:T(8,128)S(1)} %get-tuple-element.63), channel_id=1, replica_groups=mesh['grp'=4,'blk'=8] {'blk'}, dimensions={0} | all-to-all | bytes 131072 | tf_op jit(solution)/shard_map/all_to_all | solution.py:515
  48.6 0.9 shard_map.89
  49.5 12.5 %all_to_all.88.recv_ref = f32[32,8,256]{2,1,0:T(8,128)S(1)} all-to-all(f32[32,8,256]{2,1,0:T(8,128)S(1)} %get-tuple-element.66), channel_id=1, replica_groups=mesh['grp'=4,'blk'=8] {'grp','blk'}, dimensions={0} | all-to-all | bytes 524288 | tf_op jit(solution)/shard_map/all_to_all | solution.py:515
  62.0 1.2 shard_map.90
  63.2 10.0 %all_to_all.89.group_ref = f32[8,8,384]{2,1,0:T(8,128)S(1)} all-to-all(f32[8,8,384]{2,1,0:T(8,128)S(1)} %get-tuple-element.69), channel_id=1, replica_groups=mesh['grp'=4,'blk'=8] {'blk'}, dimensions={0} | all-to-all | bytes 196608 | tf_op jit(solution)/shard_map/all_to_all | solution.py:515
  73.9 9.3 %all_to_all.90.group_ref = f32[8,8,256]{2,1,0:T(8,128)S(1)} all-to-all(f32[8,8,256]{2,1,0:T(8,128)S(1)} %get-tuple-element.71), channel_id=1, replica_groups=mesh['grp'=4,'blk'=8] {'blk'}, dimensions={0} | all-to-all | bytes 131072 | tf_op jit(solution)/shard_map/all_to_all | solution.py:515
  83.2 0.9 shard_map.92
  84.1 12.4 %all_to_all.91.recv_ref = f32[32,8,256]{2,1,0:T(8,128)S(1)} all-to-all(f32[32,8,256]{2,1,0:T(8,128)S(1)} %get-tuple-element.73), channel_id=1, replica_groups=mesh['grp'=4,'blk'=8] {'grp','blk'}, dimensions={0} | all-to-all | bytes 524288 | tf_op jit(solution)/shard_map/all_to_all | solution.py:515
  96.5 1.1 shard_map.93
  97.6 10.0 %all_to_all.92.group_ref = f32[8,8,384]{2,1,0:T(8,128)S(1)} all-to-all(f32[8,8,384]{2,1,0:T(8,128)S(1)} %get-tuple-element.77), channel_id=1, replica_groups=mesh['grp'=4,'blk'=8] {'blk'}, dimensions={0} | all-to-all | bytes 196608 | tf_op jit(solution)/shard_map/all_to_all | solution.py:515
  108.3 9.3 %all_to_all.93.group_ref = f32[8,8,256]{2,1,0:T(8,128)S(1)} all-to-all(f32[8,8,256]{2,1,0:T(8,128)S(1)} %get-tuple-element.79), channel_id=1, replica_groups=mesh['grp'=4,'blk'=8] {'blk'}, dimensions={0} | all-to-all | bytes 131072 | tf_op jit(solution)/shard_map/all_to_all | solution.py:515
  117.6 0.9 shard_map.95
  118.5 12.4 %all_to_all.94.recv_ref = f32[32,8,256]{2,1,0:T(8,128)S(1)} all-to-all(f32[32,8,256]{2,1,0:T(8,128)S(1)} %get-tuple-element.81), channel_id=1, replica_groups=mesh['grp'=4,'blk'=8] {'grp','blk'}, dimensions={0} | all-to-all | bytes 524288 | tf_op jit(solution)/shard_map/all_to_all | solution.py:515
  130.8 1.2 shard_map.96
  132.0 10.0 %all_to_all.95.group_ref = f32[8,8,384]{2,1,0:T(8,128)S(1)} all-to-all(f32[8,8,384]{2,1,0:T(8,128)S(1)} %get-tuple-element.85), channel_id=1, replica_groups=mesh['grp'=4,'blk'=8] {'blk'}, dimensions={0} | all-to-all | bytes 196608 | tf_op jit(solution)/shard_map/all_to_all | solution.py:515
  142.7 9.3 %all_to_all.96.group_ref = f32[8,8,256]{2,1,0:T(8,128)S(1)} all-to-all(f32[8,8,256]{2,1,0:T(8,128)S(1)} %get-tuple-element.87), channel_id=1, replica_groups=mesh['grp'=4,'blk'=8] {'blk'}, dimensions={0} | all-to-all | bytes 131072 | tf_op jit(solution)/shard_map/all_to_all | solution.py:515
  152.0 0.9 shard_map.98
  152.9 12.4 %all_to_all.97.recv_ref = f32[32,8,256]{2,1,0:T(8,128)S(1)} all-to-all(f32[32,8,256]{2,1,0:T(8,128)S(1)} %get-tuple-element.89), channel_id=1, replica_groups=mesh['grp'=4,'blk'=8] {'grp','blk'}, dimensions={0} | all-to-all | bytes 524288 | tf_op jit(solution)/shard_map/all_to_all | solution.py:515
  165.2 1.2 shard_map.99
  166.4 10.0 %all_to_all.98.group_ref = f32[8,8,384]{2,1,0:T(8,128)S(1)} all-to-all(f32[8,8,384]{2,1,0:T(8,128)S(1)} %get-tuple-element.93), channel_id=1, replica_groups=mesh['grp'=4,'blk'=8] {'blk'}, dimensions={0} | all-to-all | bytes 196608 | tf_op jit(solution)/shard_map/all_to_all | solution.py:515
  177.1 9.3 %all_to_all.99.group_ref = f32[8,8,256]{2,1,0:T(8,128)S(1)} all-to-all(f32[8,8,256]{2,1,0:T(8,128)S(1)} %get-tuple-element.95), channel_id=1, replica_groups=mesh['grp'=4,'blk'=8] {'blk'}, dimensions={0} | all-to-all | bytes 131072 | tf_op jit(solution)/shard_map/all_to_all | solution.py:515
  186.4 0.9 shard_map.101
  187.3 12.4 %all_to_all.100.recv_ref = f32[32,8,256]{2,1,0:T(8,128)S(1)} all-to-all(f32[32,8,256]{2,1,0:T(8,128)S(1)} %get-tuple-element.97), channel_id=1, replica_groups=mesh['grp'=4,'blk'=8] {'grp','blk'}, dimensions={0} | all-to-all | bytes 524288 | tf_op jit(solution)/shard_map/all_to_all | solution.py:515
  199.7 1.7 shard_map.102
  201.3 9.8 %all_to_all.101.dots_ref = f32[32,8,128]{2,1,0:T(8,128)S(1)} all-to-all(f32[32,8,128]{2,1,0:T(8,128)S(1)} %get-tuple-element.101), channel_id=1, replica_groups=mesh['grp'=4,'blk'=8] {'grp','blk'}, dimensions={0} | all-to-all | bytes 262144 | tf_op jit(solution)/shard_map/all_to_all | solution.py:515
  (16 shorter events, 4.4 us)
Async XLA Ops:
  2.7 8.6 %collective-permute-start = (f32[72,128]{1,0:T(8,128)}, f32[72,128]{1,0:T(8,128)S(1)}, u32[]{:S(2)}, u32[]{:S(2)}) collective-permute-start(f32[72,128]{1,0:T(8,128)} %shard_map.86), channel_id=1, source_target_pairs={{0,1},{1,2},{2,3},{3,4},{4,5},{5,6},{6,7},{7,8},{8,9},{9,10},{10,1... | collective-permute-start | bytes 110600 | tf_op jit(solution)/shard_map/ppermute | solution.py:531
  11.3 14.4 %copy-start.2 = (f32[8,256]{1,0:T(8,128)S(1)}, f32[8,256]{1,0:T(8,128)}, u32[]{:S(2)}) copy-start(f32[8,256]{1,0:T(8,128)} %vector_ref.5) | copy-start | bytes 24580
  11.3 14.4 %copy-start.3 = (f32[72,128]{1,0:T(8,128)S(1)}, f32[72,128]{1,0:T(8,128)}, u32[]{:S(2)}) copy-start(f32[72,128]{1,0:T(8,128)} %get-tuple-element.58.own_ref) | copy-start | bytes 110596
  11.3 14.4 %copy-start.4 = (f32[8,256]{1,0:T(8,128)S(1)}, f32[8,256]{1,0:T(8,128)}, u32[]{:S(2)}) copy-start(f32[8,256]{1,0:T(8,128)} %cond_ref.1) | copy-start | bytes 24580
  28.5 10.1 %copy-start = (s32[16,8,256]{2,1,0:T(8,128)S(1)}, s32[16,8,256]{2,1,0:T(8,128)}, u32[]{:S(2)}) copy-start(s32[16,8,256]{2,1,0:T(8,128)} %get-tuple-element.62.near_ref.refs_2_) | copy-start | bytes 393220
  49.5 12.5 %copy-start.1 = (s32[8,8,256]{2,1,0:T(8,128)S(1)}, s32[8,8,256]{2,1,0:T(8,128)}, u32[]{:S(2)}) copy-start(s32[8,8,256]{2,1,0:T(8,128)} %get-tuple-element.68.refs_3_) | copy-start | bytes 196612
